TPU v7x, 512 devices: a whole 4x4x16 slice. The times are simulated.
512 devices in a mesh: chan: 16 (over z_lo, core), tok: 32 (over z_hi, y, x).
Axes of the slice: x: 4, y: 4, z: 16 (z_hi: 2, z_lo: 8; z = z_hi * 8 + z_lo), core: 2. Of those that a mesh axis runs over, the one named last changes fastest.
Arguments:
- codes: bfloat16 [38400, 16384], P('tok', 'chan'), may hold values from -6 to 6
- scale_exp: int32 [16384], P('chan'), may hold values from -2 to 2
- delta: bfloat16 [38400, 16384], P('tok', 'chan'), may hold values from -4 to 4
Outputs:
- gram: float32 [16384, 512], P(('chan', 'tok'))
- mismatch: float32 [16384, 512], P(('chan', 'tok'))
All inputs are finite; a program needn't handle non-finite values.
Results may differ from a plain program's by a relative error of at most 0.0003.
Values may be sent and summed in bfloat16 or wider, within the bound.
A program may use at most 64 MiB of HBM per device.

v0:
```python
import jax
import jax.numpy as jnp
from jax import lax
from jax.sharding import Mesh
from jax.sharding import PartitionSpec as P

WCOL = 32
TOK = ("tok_0", "tok_1", "tok_2")
CHAN_TOK = ("chan", "tok_0", "tok_1", "tok_2")


def in_order(blocks, dim):
    blocks = jnp.moveaxis(blocks, 0, dim)
    shape = blocks.shape
    return blocks.reshape(*shape[:dim], shape[dim] * shape[dim + 1], *shape[dim + 2 :])


def from_everyone(value, axis):
    size = lax.axis_size(axis)
    return lax.all_to_all(
        jnp.broadcast_to(value[None], (size, *value.shape)), axis, 0, 0, tiled=True
    )


def gather_directly(value, axis, dim):
    return in_order(from_everyone(value, axis), dim)


def own_block(blocks, axes, sequence):
    shape = [lax.axis_size(a) for a in axes]
    blocks = blocks.reshape(*shape, *blocks.shape[1:])
    blocks = blocks.transpose(*sequence, *range(len(axes), blocks.ndim))
    blocks = blocks.reshape(-1, *blocks.shape[len(axes) :])
    for k in sequence:
        blocks = lax.psum_scatter(blocks, axes[k], scatter_dimension=0, tiled=True)
    return blocks[0]


def in_blocks(value, dim, size):
    before, after = (value.shape[:dim], value.shape[dim + 1 :])
    return jnp.moveaxis(value.reshape(*before, size, -1, *after), dim, 0)


def sum_by_axis(value, axes, sequence, dim):
    size = lax.axis_size(axes)
    return own_block(in_blocks(value, dim, size), axes, sequence)


def cross(left, right):
    return lax.dot_general(
        left, right, (((0,), (0,)), ((), ())), preferred_element_type=jnp.float32
    )


def shards(codes, scale_exp, delta):
    scale = jnp.exp2(scale_exp.astype(jnp.float32)).astype(jnp.bfloat16)
    xq = codes * scale[None, :]
    local_win = xq[:, :WCOL]
    total = codes.shape[0] * lax.axis_size(TOK)
    gram_factor = 1.0 / jnp.float32(total)
    mis_factor = 1.0 / jnp.sqrt(jnp.float32(total))
    piece = gather_directly(local_win, "chan", 1)
    both = jnp.stack([cross(xq, piece), cross(delta, piece)])
    summed = sum_by_axis(both, TOK, (1, 2, 0), 1)
    gram = summed[0] * gram_factor
    mismatch = summed[1] * mis_factor
    return (gram, mismatch)


def solution(mesh):
    split = Mesh(
        mesh.devices.reshape(mesh.shape["chan"], 2, 4, 4), ("chan", "tok_0", "tok_1", "tok_2")
    )
    in_specs = (P(TOK, "chan"), P("chan"), P(TOK, "chan"))
    out_specs = (P(CHAN_TOK, None), P(CHAN_TOK, None))
    return jax.shard_map(
        shards, mesh=split, in_specs=in_specs, out_specs=out_specs, check_vma=False
    )
```

profile of v0, /device:TPU:1, one launch (start us, length us, event | category | flops | bytes accessed | tf_op | source)
XLA Modules:
  0.0 240.0 jit_solution(14414883931784663099)
XLA Ops:
  7.2 0.0 copy-start
  7.2 0.0 reduce-scatter.4.cloned.1.call-start
  7.2 0.8 exponential_convert_fusion
  8.1 4.4 %copy.8 = bf16[1200,1024]{0,1:T(8,128)(2,1)} copy(bf16[1200,1024]{1,0:T(8,128)(2,1)} %param.3) | data formatting | bytes 4915200 | tf_op args[0]
  12.4 2.0 broadcast_multiply_fusion
  14.4 0.0 copy-start.2
  14.4 0.1 broadcast_in_dim.2
  14.6 75.9 %all_to_all.5 = bf16[16,1200,32]{1,2,0:T(8,128)(2,1)S(1)} all-to-all(bf16[16,1200,32]{1,2,0:T(8,128)(2,1)S(1)} %broadcast_in_dim.2), channel_id=1, replica_groups=mesh['chan'=16,'tok_0'=2,'tok_1'=4,'tok_2'=4] {'chan'}, dimensions={0} | all-to-all | bytes 2457600 | tf_op jit(solution)/shard_map/all_to_all | solution.py:20
  90.5 0.0 copy-done.2
  90.5 0.0 copy-start.3
  90.5 1.1 copy-done.3
  91.5 0.0 copy-done
  91.5 2.9 %convolution_bitcast_fusion = f32[1024,512]{0,1:T(8,128)} fusion(bf16[1200,512]{0,1:T(8,128)(2,1)S(1)} %bitcast.31, bf16[1200,1024]{1,0:T(8,128)(2,1)S(1)} %copy-done), kind=kOutput, calls=%fused_computation.1 | convolution fusion | flops 1258291200 | bytes 5783552 | tf_op jit(solution)/shard_map/dot_general | solution.py:50
  94.5 2.9 %copy.10 = f32[1024,512]{1,0:T(8,128)} copy(f32[1024,512]{0,1:T(8,128)} %convolution_bitcast_fusion) | data formatting | bytes 4194304 | tf_op jit(solution)/shard_map/dot_general | solution.py:50
  97.4 0.0 copy-start.1
  97.4 3.8 %convolution_bitcast_fusion.1 = f32[1,32,32,512]{3,2,1,0:T(8,128)S(1)} fusion(bf16[32,32,1200]{2,1,0:T(8,128)(2,1)} %bitcast.30, bf16[1200,512,1]{0,1,2:T(8,128)(2,1)} %bitcast.32), kind=kOutput, calls=%fused_computation.2 | convolution fusion | flops 1258291200 | bytes 5783552 | tf_op jit(solution)/shard_map/dot_general | solution.py:50
  101.2 0.0 copy-done.1
  101.2 0.8 pad_maximum_fusion
  102.0 2.4 %copy.11 = f32[4,4,2,2,32,512]{5,4,3,2,1,0:T(8,128)} copy(f32[4,4,2,2,32,512]{5,4,1,0,2,3:T(8,128)S(1)} %bitcast.28) | data formatting | bytes 8388608 | tf_op jit(solution)/shard_map/transpose | solution.py:32
  104.4 0.0 reduce-scatter.4.cloned.1.call-update
  104.5 0.0 reduce-scatter.6.cloned.1.call-start
  104.5 51.1 %reduce-scatter.4.cloned.1.call-done = f32[8,2,32,512]{3,2,1,0:T(8,128)} async-done(((f32[32,2,32,512]{3,2,1,0:T(8,128)}), f32[8,2,32,512]{3,2,1,0:T(8,128)}) %reduce-scatter.4.cloned.1.call-update) | async-done | bytes 1048592 | tf_op jit(solution)/shard_map/reduce_scatter | solution.py:35
  155.6 0.0 reduce-scatter.6.cloned.1.call-update
  155.6 0.0 reduce-scatter.8.cloned.1.call-start
  155.7 31.9 %reduce-scatter.6.cloned.1.call-done = f32[2,2,32,512]{3,2,1,0:T(8,128)} async-done(((f32[8,2,32,512]{3,2,1,0:T(8,128)}), f32[2,2,32,512]{3,2,1,0:T(8,128)}) %reduce-scatter.6.cloned.1.call-update) | async-done | bytes 262160 | tf_op jit(solution)/shard_map/reduce_scatter | solution.py:35
  187.6 0.0 reduce-scatter.8.cloned.1.call-update
  187.6 44.3 %reduce-scatter.8.cloned.1.call-done = f32[1,2,32,512]{3,2,1,0:T(8,128)} async-done(((f32[2,2,32,512]{3,2,1,0:T(8,128)}), f32[1,2,32,512]{3,2,1,0:T(8,128)}) %reduce-scatter.8.cloned.1.call-update) | async-done | bytes 131088 | tf_op jit(solution)/shard_map/reduce_scatter | solution.py:35
  232.0 1.5 fusion
  (1 shorter events, 0.0 us)
Async XLA Ops:
  7.2 84.4 %copy-start = (bf16[1200,1024]{1,0:T(8,128)(2,1)S(1)}, bf16[1200,1024]{1,0:T(8,128)(2,1)}, u32[]{:S(2)}) copy-start(bf16[1200,1024]{1,0:T(8,128)(2,1)} %param.5) | copy-start | bytes 7372804
  7.2 148.4 %reduce-scatter.4.cloned.1.call-start = ((), (), s32[]{:S(2)}) async-start(), calls=%async_computation.4 | async-start | bytes 5242880 | tf_op jit(solution)/shard_map/reduce_scatter | solution.py:35
  14.4 76.1 %copy-start.2 = (bf16[1200,1024]{0,1:T(8,128)(2,1)}, bf16[1200,1024]{0,1:T(8,128)(2,1)S(1)}, u32[]{:S(2)}) copy-start(bf16[1200,1024]{0,1:T(8,128)(2,1)S(1)} %broadcast_multiply_fusion) | copy-start | bytes 7372804
  90.5 1.1 copy-start.3
  97.4 3.8 %copy-start.1 = (f32[1024,512]{1,0:T(8,128)S(1)}, f32[1024,512]{1,0:T(8,128)}, u32[]{:S(2)}) copy-start(f32[1024,512]{1,0:T(8,128)} %copy.10) | copy-start | bytes 6291460
  104.5 83.1 %reduce-scatter.6.cloned.1.call-start = ((), (), s32[]{:S(2)}) async-start(), calls=%async_computation.5 | async-start | bytes 1310720 | tf_op jit(solution)/shard_map/reduce_scatter | solution.py:35
  155.6 76.3 %reduce-scatter.8.cloned.1.call-start = ((), (), s32[]{:S(2)}) async-start(), calls=%async_computation.6 | async-start | bytes 393216 | tf_op jit(solution)/shard_map/reduce_scatter | solution.py:35
Sparse Core Ops, SparseCore 0:
  104.6 50.9 reduce-scatter.3
  158.7 28.8 reduce-scatter.5
  190.4 41.5 reduce-scatter.7
where the time goes:
time: 240 us
  waiting for transfers between devices  127 us (53%)
  blocking collectives  75.9 us (32%)
  between operations  13.8 us (6%)
  local copies, waits for them, and re-layouts  10.9 us (5%)
  matrix products  6.72 us (3%)
  other arithmetic  5.15 us (2%)
    reduce_scatter x3, waiting for transfers between devices, own_block(): blocks = lax.psum_scatter(blocks, axes[k], scatter_dimension=0, tiled=True)  127 us
    all_to_all x1, blocking collectives, from_everyone(): lax.all_to_all(jnp.broadcast_to(value[None], (size, *value.shape)), axis,...  75.9 us
    dot_general x2, matrix products, cross(): lax.dot_general(left, right, (((0,), (0,)), ((), ())), preferred_element_...  6.72 us
    unnamed x9, local copies, waits for them, and re-layouts  5.43 us
  transfers between devices with their start and end apart: 3, of which 3 were waited for; matrix products, arithmetic and copies ran while one was open for 0% of the time, Pallas kernels for 0%

commit v1 on v0

v1 whole, which is shorter than its diff:
```python
import functools

import jax
import jax.numpy as jnp
from jax import lax
from jax.experimental import pallas as pl
from jax.experimental.pallas import tpu as pltpu
from jax.sharding import Mesh
from jax.sharding import PartitionSpec as P

WCOL = 32
AXES = ("zlo", "core", "zhi", "y", "x")
TOK = ("zhi", "y", "x")
MESH = pl.DeviceIdType.MESH
F32, BF16, I32, I16 = jnp.float32, jnp.bfloat16, jnp.int32, jnp.int16

DIRECT = {
    0: (1, 4), 1: (0, 2, 5), 2: (1, 3, 6), 3: (2, 4, 1, 6),
    4: (3, 1, 6), 5: (4, 1, 6), 6: (5, 7, 2), 7: (6, 3),
}
RELAY = {
    0: {},
    1: {0: (2,), 2: (0,), 3: (0,), 4: (0, 2), 5: (0, 2)},
    2: {1: (3,), 6: (0, 1, 3)},
    3: {2: (4,), 7: (0, 1, 2, 4)},
    4: {0: (3, 5, 6, 7), 3: (5,), 5: (3,)},
    5: {1: (4, 6, 7), 6: (4,)},
    6: {2: (5, 7), 3: (7,), 4: (5, 7), 5: (7,), 7: (5,)},
    7: {},
}
TAKE = {
    0: (1, 2, 3, 4, 5, 6, 7), 1: (2, 0, 3, 4, 5, 6, 7), 2: (3, 1, 6, 0, 7, 4, 5), 3: (2, 4, 7, 5, 6, 1, 0),
    4: (5, 3, 0, 2, 1, 6, 7), 5: (4, 6, 1, 7, 3, 2, 0), 6: (7, 5, 4, 3, 2, 0, 1), 7: (6, 5, 4, 3, 2, 1, 0),
}
CHUNKS = {
    0: (0, 1, 2, 3), 1: (0, 1, 2, 3), 2: (1, 0, 3, 2), 3: (1, 2, 3, 0),
    4: (2, 1, 0, 3), 5: (2, 3, 1, 0), 6: (3, 2, 1, 0), 7: (3, 2, 1, 0),
}
STEPS = ((0, 1), (2, 3), (4, 5), (6,))
TOP = 32000.0


def coded(value, groups):
    blocks = value.reshape(groups, 32, 128)
    largest = jnp.maximum(jnp.max(jnp.abs(blocks), axis=1), 2.0**-110)
    eighths = jnp.ceil(jnp.log2(largest) * 8.0)
    factor = jnp.exp2(eighths * -0.125) * TOP
    whole = jnp.round(blocks * factor[:, None, :]).astype(I32).astype(I16)
    if groups < 16:
        eighths = jnp.concatenate([eighths, jnp.zeros((16 - groups, 128), F32)], axis=0)
    return whole.reshape(groups * 32, 128), eighths.astype(I32).astype(I16)


def decoded(ref, at, groups):
    rows = groups * 32
    whole = ref[(*at, pl.ds(0, rows), slice(None))].astype(I32).astype(F32)
    eighths = ref[(*at, pl.ds(rows, 16), slice(None))].astype(I32).astype(F32)[:groups]
    factor = jnp.exp2(eighths * 0.125) * (1.0 / TOP)
    return (whole.reshape(groups, 32, 128) * factor[:, None, :]).reshape(rows, 128)


def kernel(total, codes, scale_exp, delta, gram, mismatch, xs, ds, scale, left, win, own1, own2,
           s1, r1, s2, r2, s3, r3, load_sem, wsend, wrecv, csend, crecv, q1s, q1r, q2s, q2r, q3s, q3r, go_sem):
    tokens, width = codes.shape
    padded = xs.shape[0]
    zlo, core, zhi, y, x = (lax.axis_index(a) for a in AXES)
    z = zhi * 8 + zlo

    def along(d):
        n = lax.rem(z + (d + 16), 16)
        return {"zhi": n // 8, "zlo": lax.rem(n, 8)}

    loads = [
        pltpu.make_async_copy(codes.at[:, pl.ds(0, 128)], xs.at[pl.ds(0, tokens), pl.ds(0, 128)], load_sem.at[0]),
        pltpu.make_async_copy(scale_exp, scale, load_sem.at[1]),
        pltpu.make_async_copy(codes.at[:, pl.ds(128, width - 128)], xs.at[pl.ds(0, tokens), pl.ds(128, width - 128)], load_sem.at[2]),
        pltpu.make_async_copy(delta, ds.at[pl.ds(0, tokens)], load_sem.at[3]),
    ]
    for c in loads:
        c.start()
    barrier = pltpu.get_barrier_semaphore()
    greet = [{"core": 1 - core}]
    greet += [along(d) for d in (1, -1, 2, -2, 3, -3, 4, -4)]
    greet += [{a: lax.rem(lax.axis_index(a) + k, 4)} for a in ("x", "y") for k in (1, 2, 3)]
    for who in greet:
        pl.semaphore_signal(barrier, inc=1, device_id=who, device_id_type=MESH)

    xs[pl.ds(tokens, padded - tokens), :] = jnp.zeros((padded - tokens, width), BF16)
    ds[pl.ds(tokens, padded - tokens), :] = jnp.zeros((padded - tokens, width), BF16)
    loads[0].wait()
    loads[1].wait()

    def factors(i):
        return jnp.exp2(scale[pl.ds(i, 1), :].astype(F32)).astype(BF16)

    my_rows = pl.ds(pl.multiple_of((zlo * 2 + core) * WCOL, WCOL), WCOL)
    win[my_rows, :] = (xs[:, pl.ds(0, 128)] * factors(0)).T[:WCOL]

    loads[2].wait()
    loads[3].wait()

    def place(i, stat, block):
        hi, row = i // 4, lax.rem(i, 4)
        for k in range(4):
            first = jnp.where(hi == 0, k * 4 + row, row * 4 + k)
            start = pl.multiple_of(hi * width + (first * 2 + stat) * 32, 32)
            left[pl.ds(start, 32), :] = block[k * 32 : (k + 1) * 32]

    @pl.loop(0, width // 128)
    def _(i):
        lanes = pl.ds(pl.multiple_of(i * 128, 128), 128)
        place(i, 0, (xs[:, lanes] * factors(i)).T)
        place(i, 1, ds[:, lanes].T)

    pl.semaphore_wait(barrier, len(greet))
    pl.semaphore_signal(go_sem, inc=1, device_id=along(4), device_id_type=MESH)

    def block_rows(s, c):
        return pl.ds(pl.multiple_of((s * 2 + c) * WCOL, WCOL), WCOL)

    def hand(s, to):
        return pltpu.make_async_remote_copy(
            src_ref=win.at[block_rows(s, core)], dst_ref=win.at[block_rows(s, core)],
            send_sem=wsend.at[s, to], recv_sem=wrecv.at[s],
            device_id={"zlo": to}, device_id_type=MESH)

    def across(s):
        return pltpu.make_async_remote_copy(
            src_ref=win.at[block_rows(s, core)], dst_ref=win.at[block_rows(s, core)],
            send_sem=csend.at[s], recv_sem=crecv.at[s],
            device_id={"core": 1 - core}, device_id_type=MESH)

    def sent_by(a):
        return [(a, to) for to in DIRECT[a]] + [(s, to) for s, tos in RELAY[a].items() for to in tos]

    across(zlo).start()
    for a in range(8):
        @pl.when(zlo == a)
        def _(a=a):
            for to in DIRECT[a]:
                hand(a, to).start()

    def take(a, n):
        s = TAKE[a][n]
        hand(s, a).wait_recv()
        for to in RELAY[a].get(s, ()):
            hand(s, to).start()
        across(s).start()

    def taken(a, n):
        across(TAKE[a][n]).wait_recv()

    def chunk_of(k):
        q = jnp.int32(0)
        for a in range(8):
            for n in range(4):
                q = jnp.where((zlo == a) & (k == n), CHUNKS[a][n], q)
        return q

    axes = (("x", "y"), ("y", "x"))

    def send1(k, h, j):
        to = lax.rem(lax.axis_index(axes[h][0]) + j + 1, 4)
        return pltpu.make_async_remote_copy(
            src_ref=s1.at[k, h, j], dst_ref=r1.at[k, h, j], send_sem=q1s.at[k, h, j], recv_sem=q1r.at[k, h, j],
            device_id={axes[h][0]: to}, device_id_type=MESH)

    def send2(k, h, j):
        to = lax.rem(lax.axis_index(axes[h][1]) + j + 1, 4)
        return pltpu.make_async_remote_copy(
            src_ref=s2.at[k, h, j], dst_ref=r2.at[k, h, j], send_sem=q2s.at[k, h, j], recv_sem=q2r.at[k, h, j],
            device_id={axes[h][1]: to}, device_id_type=MESH)

    def send3(k):
        return pltpu.make_async_remote_copy(
            src_ref=s3.at[k], dst_ref=r3.at[k], send_sem=q3s.at[k], recv_sem=q3r.at[k],
            device_id={"zhi": 1 - zhi}, device_id_type=MESH)

    def multiply(k):
        q = chunk_of(k)
        right = win[pl.ds(pl.multiple_of(q * 128, 128), 128), :]

        def tile(h, t):
            rows = pl.ds(pl.multiple_of(h * width + t * 256, 256), 256)
            return lax.dot_general(left[rows, :], right, (((1,), (1,)), ((), ())), preferred_element_type=F32)

        for h in range(2):
            me = lax.axis_index(axes[h][0])

            @pl.loop(0, 3)
            def _(j, h=h, me=me):
                whole, eighths = coded(tile(h, lax.rem(me + j + 1, 4)), 8)
                s1[k, h, j, pl.ds(0, 256), :] = whole
                s1[k, h, j, pl.ds(256, 16), :] = eighths
                send1(k, h, j).start()

            own1[k, h] = tile(h, me)

    def second(k):
        for h in range(2):
            for j in range(3):
                send1(k, h, j).wait_recv()
            me = lax.axis_index(axes[h][1])
            own1[k, h] = own1[k, h] + decoded(r1, (k, h, 0), 8) + decoded(r1, (k, h, 1), 8) + decoded(r1, (k, h, 2), 8)
            for j in range(3):
                t = lax.rem(me + j + 1, 4)
                whole, eighths = coded(own1[k, h, pl.ds(pl.multiple_of(t * 64, 64), 64), :], 2)
                s2[k, h, j, pl.ds(0, 64), :] = whole
                s2[k, h, j, pl.ds(64, 16), :] = eighths
                send2(k, h, j).start()
            own2[k, h] = own1[k, h, pl.ds(pl.multiple_of(me * 64, 64), 64), :]

    def third(k):
        for h in range(2):
            for j in range(3):
                send2(k, h, j).wait_recv()
            own2[k, h] = own2[k, h] + decoded(r2, (k, h, 0), 2) + decoded(r2, (k, h, 1), 2) + decoded(r2, (k, h, 2), 2)
        whole, eighths = coded(own2[k, 1 - zhi], 2)
        s3[k, pl.ds(0, 64), :] = whole
        s3[k, pl.ds(64, 16), :] = eighths
        send3(k).start()

    def last(k):
        send3(k).wait_recv()
        result = own2[k, zhi] + decoded(r3, (k,), 2)
        lanes = pl.ds(pl.multiple_of(chunk_of(k) * 128, 128), 128)
        gram[:, lanes] = result[:32] * (1.0 / total)
        mismatch[:, lanes] = result[32:] * (1.0 / total**0.5)

    @pl.loop(0, 7)
    def _(phase):
        for n in range(4):
            for a in range(8):
                @pl.when((phase == n) & (zlo == a))
                def _(n=n, a=a):
                    for e in STEPS[n]:
                        take(a, e)
                    if n == 0:
                        across(a).wait_recv()
                    for e in STEPS[n]:
                        taken(a, e)

        @pl.when(phase < 4)
        def _():
            multiply(phase)

        @pl.when((phase >= 1) & (phase < 5))
        def _():
            second(phase - 1)

        @pl.when(phase == 2)
        def _():
            pl.semaphore_wait(go_sem, 1)

        @pl.when((phase >= 2) & (phase < 6))
        def _():
            third(phase - 2)

        @pl.when(phase >= 3)
        def _():
            last(phase - 3)

    for a in range(8):
        @pl.when(zlo == a)
        def _(a=a):
            for s, to in sent_by(a):
                hand(s, to).wait_send()

    @pl.loop(0, 8)
    def _(s):
        across(s).wait_send()

    @pl.loop(0, 4)
    def _(k):
        for h in range(2):
            for j in range(3):
                send1(k, h, j).wait_send()
                send2(k, h, j).wait_send()
        send3(k).wait_send()


def shards(codes, scale_exp, delta):
    tokens, width = codes.shape
    total = float(tokens * lax.axis_size(TOK))
    padded = -(-tokens // 128) * 128
    dma = pltpu.SemaphoreType.DMA
    return pl.pallas_call(
        functools.partial(kernel, total),
        out_shape=(jax.ShapeDtypeStruct((32, 512), F32), jax.ShapeDtypeStruct((32, 512), F32)),
        in_specs=[pl.BlockSpec(memory_space=pl.ANY)] * 3,
        out_specs=(pl.BlockSpec(memory_space=pltpu.VMEM),) * 2,
        scratch_shapes=[
            pltpu.VMEM((padded, width), BF16),
            pltpu.VMEM((padded, width), BF16),
            pltpu.VMEM((8, 128), I32),
            pltpu.VMEM((2 * width, padded), BF16),
            pltpu.VMEM((512, padded), BF16),
            pltpu.VMEM((4, 2, 256, 128), F32),
            pltpu.VMEM((4, 2, 64, 128), F32),
            pltpu.VMEM((4, 2, 3, 272, 128), I16),
            pltpu.VMEM((4, 2, 3, 272, 128), I16),
            pltpu.VMEM((4, 2, 3, 80, 128), I16),
            pltpu.VMEM((4, 2, 3, 80, 128), I16),
            pltpu.VMEM((4, 80, 128), I16),
            pltpu.VMEM((4, 80, 128), I16),
            dma((4,)),
            dma((8, 8)),
            dma((8,)),
            dma((8,)),
            dma((8,)),
            dma((4, 2, 3)),
            dma((4, 2, 3)),
            dma((4, 2, 3)),
            dma((4, 2, 3)),
            dma((4,)),
            dma((4,)),
            pltpu.SemaphoreType.REGULAR,
        ],
        compiler_params=pltpu.CompilerParams(
            collective_id=0, has_side_effects=True, vmem_limit_bytes=56 * 2**20
        ),
        cost_estimate=pl.CostEstimate(
            flops=2 * 2 * width * 512 * tokens, bytes_accessed=4 * tokens * width, transcendentals=0
        ),
    )(codes, scale_exp.reshape(width // 128, 128), delta)


def solution(mesh):
    split = Mesh(mesh.devices.reshape(8, 2, 2, 4, 4), AXES)
    chan = ("zlo", "core")
    return jax.shard_map(
        shards,
        mesh=split,
        in_specs=(P(TOK, chan), P(chan), P(TOK, chan)),
        out_specs=(P((*chan, *TOK), None), P((*chan, *TOK), None)),
        check_vma=False,
    )
```

time: 240 us -> 68.4 us (0.29)
  waiting for transfers between devices: 127 us -> 0 us
  blocking collectives: 75.9 us -> 0 us
  Pallas kernels: 0 us -> 64.6 us
  between operations: 13.8 us -> 0.64 us
  local copies, waits for them, and re-layouts: 10.9 us -> 2.95 us
  matrix products: 6.72 us -> 0 us
  other arithmetic: 5.15 us -> 0 us
    reduce_scatter x3 -> x0, waiting for transfers between devices: 127 us -> none  [own_block(): blocks = lax.psum_scatter(blocks, axes[k], scatter_dimension=0, tiled=True)]
    all_to_all x1 -> x0, blocking collectives: 75.9 us -> none  [from_everyone(): lax.all_to_all(jnp.broadcast_to(value[None], (size, *value.shape)), axis,...]
    pallas_call x0 -> x1, Pallas kernels: none -> 64.6 us  [shards(): pl.pallas_call(functools.partial(kernel, total), out_shape=(jax.ShapeDtyp...]
    dot_general x2 -> x0, matrix products: 6.72 us -> none  [cross(): lax.dot_general(left, right, (((0,), (0,)), ((), ())), preferred_element_...]
    mul x2 -> x0, other arithmetic: 3.5 us -> none  [the longest x1 1.97 us: shards(): xq = codes * scale[None, :]]
    dot_general x1 -> x0, local copies, waits for them, and re-layouts: 2.9 us -> none  [cross(): lax.dot_general(left, right, (((0,), (0,)), ((), ())), preferred_element_...]
    unnamed x9 -> x2, local copies, waits for them, and re-layouts: 5.43 us -> 2.95 us
    transpose x1 -> x0, local copies, waits for them, and re-layouts: 2.44 us -> none  [own_block(): blocks = blocks.transpose(*sequence, *range(len(axes), blocks.ndim))]
  transfers between devices with their start and end apart: 3 -> 0, of which waited for: 3 -> 0; matrix products, arithmetic and copies ran while one was open for 0% -> 0% of each run, Pallas kernels for 0% -> 0%
where the time goes in v1:
time: 68.4 us; the launch traced here: 68.2 us
  Pallas kernels  64.6 us (94%)
  local copies, waits for them, and re-layouts  2.95 us (4%)
    pallas_call x1, Pallas kernels, shards(): pl.pallas_call(functools.partial(kernel, total), out_shape=(jax.ShapeDtyp...  64.6 us
    unnamed x2, local copies, waits for them, and re-layouts  2.95 us

profile of v1, /device:TPU:1, one launch (start us, length us, event | category | flops | bytes accessed | tf_op | source)
XLA Modules:
  0.0 68.2 jit_solution(6382977569330037401)
XLA Ops:
  0.6 64.6 %shard_map.50 = (f32[32,512]{1,0:T(8,128)}, f32[32,512]{1,0:T(8,128)}) custom-call(bf16[1200,1024]{1,0:T(8,128)(2,1)} %codes.1, s32[8,128]{1,0:T(8,128)} %bitcast.1, bf16[1200,1024]{1,0:T(8,128)(2,1)} %delta.1), custom_call_target="tpu_custom_call" | custom-call | flops 2516582400 | bytes 4915200 | tf_op jit(solution)/shard_map/pallas_call | solution.py:287
  65.2 1.5 %copy.7 = f32[32,512]{1,0:T(8,128)} copy(f32[32,512]{1,0:T(8,128)} %get-tuple-element.4) | data formatting | bytes 131072
  66.7 1.5 %copy.8 = f32[32,512]{1,0:T(8,128)} copy(f32[32,512]{1,0:T(8,128)} %get-tuple-element.5) | data formatting | bytes 131072

commit v2 on v1

--- a/solution.py
+++ b/solution.py
@@ -15,28 +15,36 @@
 F32, BF16, I32, I16 = jnp.float32, jnp.bfloat16, jnp.int32, jnp.int16
 
 DIRECT = {
-    0: (1, 4), 1: (0, 2, 5), 2: (1, 3, 6), 3: (2, 4, 1, 6),
-    4: (3, 1, 6), 5: (4, 1, 6), 6: (5, 7, 2), 7: (6, 3),
+    0: (4, 1),
+    1: (5, 2, 0),
+    2: (6, 1, 3),
+    3: (6, 1, 4, 2),
+    4: (1, 6, 3),
+    5: (1, 4, 6),
+    6: (2, 5, 7),
+    7: (3, 6),
 }
 RELAY = {
     0: {},
     1: {0: (2,), 2: (0,), 3: (0,), 4: (0, 2), 5: (0, 2)},
     2: {1: (3,), 6: (0, 1, 3)},
     3: {2: (4,), 7: (0, 1, 2, 4)},
-    4: {0: (3, 5, 6, 7), 3: (5,), 5: (3,)},
-    5: {1: (4, 6, 7), 6: (4,)},
-    6: {2: (5, 7), 3: (7,), 4: (5, 7), 5: (7,), 7: (5,)},
+    4: {3: (5,), 5: (3,), 0: (7, 6, 3, 5)},
+    5: {6: (4,), 1: (7, 4, 6)},
+    6: {5: (7,), 7: (5,), 4: (5, 7), 3: (7,), 2: (5, 7)},
     7: {},
 }
-TAKE = {
-    0: (1, 2, 3, 4, 5, 6, 7), 1: (2, 0, 3, 4, 5, 6, 7), 2: (3, 1, 6, 0, 7, 4, 5), 3: (2, 4, 7, 5, 6, 1, 0),
-    4: (5, 3, 0, 2, 1, 6, 7), 5: (4, 6, 1, 7, 3, 2, 0), 6: (7, 5, 4, 3, 2, 0, 1), 7: (6, 5, 4, 3, 2, 1, 0),
+CHUNKS = {
+    0: (0, 1, 2, 3),
+    1: (0, 1, 2, 3),
+    2: (1, 0, 2, 3),
+    3: (1, 2, 0, 3),
+    4: (2, 1, 3, 0),
+    5: (2, 3, 1, 0),
+    6: (3, 2, 1, 0),
+    7: (3, 2, 1, 0),
 }
-CHUNKS = {
-    0: (0, 1, 2, 3), 1: (0, 1, 2, 3), 2: (1, 0, 3, 2), 3: (1, 2, 3, 0),
-    4: (2, 1, 0, 3), 5: (2, 3, 1, 0), 6: (3, 2, 1, 0), 7: (3, 2, 1, 0),
-}
-STEPS = ((0, 1), (2, 3), (4, 5), (6,))
+PARTS = 5
 TOP = 32000.0
 
 
@@ -59,8 +67,8 @@
     return (whole.reshape(groups, 32, 128) * factor[:, None, :]).reshape(rows, 128)
 
 
-def kernel(total, codes, scale_exp, delta, gram, mismatch, xs, ds, scale, left, win, own1, own2,
-           s1, r1, s2, r2, s3, r3, load_sem, wsend, wrecv, csend, crecv, q1s, q1r, q2s, q2r, q3s, q3r, go_sem):
+def kernel(total, codes, scale_exp, delta, out, xs, ds, scale, left, win, product, own1, own2,
+           s1, r1, s2, r2, s3, r3, load_sem, wsend, wrecv, wpart, csend, crecv, q1s, q1r, q2s, q2r, q3s, q3r, go_sem):
     tokens, width = codes.shape
     padded = xs.shape[0]
     zlo, core, zhi, y, x = (lax.axis_index(a) for a in AXES)
@@ -96,9 +104,6 @@
     my_rows = pl.ds(pl.multiple_of((zlo * 2 + core) * WCOL, WCOL), WCOL)
     win[my_rows, :] = (xs[:, pl.ds(0, 128)] * factors(0)).T[:WCOL]
 
-    loads[2].wait()
-    loads[3].wait()
-
     def place(i, stat, block):
         hi, row = i // 4, lax.rem(i, 4)
         for k in range(4):
@@ -106,49 +111,69 @@
             start = pl.multiple_of(hi * width + (first * 2 + stat) * 32, 32)
             left[pl.ds(start, 32), :] = block[k * 32 : (k + 1) * 32]
 
+    pl.semaphore_wait(barrier, len(greet))
+    pl.semaphore_signal(go_sem, inc=1, device_id=along(4), device_id_type=MESH)
+
+    def block_rows(s, c):
+        return pl.ds(pl.multiple_of((s * 2 + c) * WCOL, WCOL), WCOL)
+
+    def hand(s, to, part=None, recv=None):
+        size = padded // PARTS
+        lanes = pl.ds(0, padded) if part is None else pl.ds(part * size, size)
+        block = win.at[block_rows(s, core), lanes]
+        return pltpu.make_async_remote_copy(
+            src_ref=block, dst_ref=block, send_sem=wsend.at[s, to], recv_sem=wrecv.at[s] if recv is None else recv,
+            device_id={"zlo": to}, device_id_type=MESH)
+
+    def across(s):
+        return pltpu.make_async_remote_copy(
+            src_ref=win.at[block_rows(s, core)], dst_ref=win.at[block_rows(s, core)],
+            send_sem=csend.at[s], recv_sem=crecv.at[s],
+            device_id={"core": 1 - core}, device_id_type=MESH)
+
+    def sent_by(a):
+        return [(a, to) for to in DIRECT[a]] + [(s, to) for s, tos in RELAY[a].items() for to in tos]
+
+    across(zlo).start()
+    for a in range(8):
+        @pl.when(zlo == a)
+        def _(a=a):
+            for part in range(PARTS):
+                for to in DIRECT[a]:
+                    if a in RELAY[to]:
+                        hand(a, to, part, wpart.at[a, part]).start()
+            for to in DIRECT[a]:
+                if a not in RELAY[to]:
+                    hand(a, to).start()
+            pass
+
+    loads[2].wait()
+    loads[3].wait()
+
     @pl.loop(0, width // 128)
     def _(i):
         lanes = pl.ds(pl.multiple_of(i * 128, 128), 128)
         place(i, 0, (xs[:, lanes] * factors(i)).T)
         place(i, 1, ds[:, lanes].T)
 
-    pl.semaphore_wait(barrier, len(greet))
-    pl.semaphore_signal(go_sem, inc=1, device_id=along(4), device_id_type=MESH)
-
-    def block_rows(s, c):
-        return pl.ds(pl.multiple_of((s * 2 + c) * WCOL, WCOL), WCOL)
-
-    def hand(s, to):
-        return pltpu.make_async_remote_copy(
-            src_ref=win.at[block_rows(s, core)], dst_ref=win.at[block_rows(s, core)],
-            send_sem=wsend.at[s, to], recv_sem=wrecv.at[s],
-            device_id={"zlo": to}, device_id_type=MESH)
-
-    def across(s):
-        return pltpu.make_async_remote_copy(
-            src_ref=win.at[block_rows(s, core)], dst_ref=win.at[block_rows(s, core)],
-            send_sem=csend.at[s], recv_sem=crecv.at[s],
-            device_id={"core": 1 - core}, device_id_type=MESH)
-
-    def sent_by(a):
-        return [(a, to) for to in DIRECT[a]] + [(s, to) for s, tos in RELAY[a].items() for to in tos]
-
-    across(zlo).start()
     for a in range(8):
         @pl.when(zlo == a)
         def _(a=a):
-            for to in DIRECT[a]:
-                hand(a, to).start()
+            for s, tos in RELAY[a].items():
+                for part in range(PARTS):
+                    hand(s, a, part, wpart.at[s, part]).wait_recv()
+                    for to in tos:
+                        hand(s, to, part).start()
+                across(s).start()
 
     def take(a, n):
-        s = TAKE[a][n]
-        hand(s, a).wait_recv()
-        for to in RELAY[a].get(s, ()):
-            hand(s, to).start()
-        across(s).start()
-
-    def taken(a, n):
-        across(TAKE[a][n]).wait_recv()
+        pair = (2 * CHUNKS[a][n], 2 * CHUNKS[a][n] + 1)
+        for s in pair:
+            if s != a and s not in RELAY[a]:
+                hand(s, a).wait_recv()
+                across(s).start()
+        for s in pair:
+            across(s).wait_recv()
 
     def chunk_of(k):
         q = jnp.int32(0)
@@ -180,21 +205,20 @@
         q = chunk_of(k)
         right = win[pl.ds(pl.multiple_of(q * 128, 128), 128), :]
 
-        def tile(h, t):
-            rows = pl.ds(pl.multiple_of(h * width + t * 256, 256), 256)
-            return lax.dot_general(left[rows, :], right, (((1,), (1,)), ((), ())), preferred_element_type=F32)
-
         for h in range(2):
             me = lax.axis_index(axes[h][0])
+            product[h] = lax.dot_general(
+                left[pl.ds(h * width, width), :], right, (((1,), (1,)), ((), ())), preferred_element_type=F32
+            ).reshape(4, width // 4, 128)
 
             @pl.loop(0, 3)
             def _(j, h=h, me=me):
-                whole, eighths = coded(tile(h, lax.rem(me + j + 1, 4)), 8)
+                whole, eighths = coded(product[h, lax.rem(me + j + 1, 4)], 8)
                 s1[k, h, j, pl.ds(0, 256), :] = whole
                 s1[k, h, j, pl.ds(256, 16), :] = eighths
                 send1(k, h, j).start()
 
-            own1[k, h] = tile(h, me)
+            own1[k, h] = product[h, me]
 
     def second(k):
         for h in range(2):
@@ -224,27 +248,19 @@
         send3(k).wait_recv()
         result = own2[k, zhi] + decoded(r3, (k,), 2)
         lanes = pl.ds(pl.multiple_of(chunk_of(k) * 128, 128), 128)
-        gram[:, lanes] = result[:32] * (1.0 / total)
-        mismatch[:, lanes] = result[32:] * (1.0 / total**0.5)
-
-    @pl.loop(0, 7)
+        out[:, lanes] = result
+
+    @pl.loop(0, 4)
     def _(phase):
         for n in range(4):
             for a in range(8):
                 @pl.when((phase == n) & (zlo == a))
                 def _(n=n, a=a):
-                    for e in STEPS[n]:
-                        take(a, e)
-                    if n == 0:
-                        across(a).wait_recv()
-                    for e in STEPS[n]:
-                        taken(a, e)
-
-        @pl.when(phase < 4)
-        def _():
-            multiply(phase)
-
-        @pl.when((phase >= 1) & (phase < 5))
+                    take(a, n)
+
+        multiply(phase)
+
+        @pl.when(phase >= 1)
         def _():
             second(phase - 1)
 
@@ -252,13 +268,17 @@
         def _():
             pl.semaphore_wait(go_sem, 1)
 
-        @pl.when((phase >= 2) & (phase < 6))
+        @pl.when(phase >= 2)
         def _():
             third(phase - 2)
 
-        @pl.when(phase >= 3)
-        def _():
-            last(phase - 3)
+    second(3)
+    third(2)
+    third(3)
+
+    @pl.loop(0, 4)
+    def _(k):
+        last(k)
 
     for a in range(8):
         @pl.when(zlo == a)
@@ -284,17 +304,18 @@
     total = float(tokens * lax.axis_size(TOK))
     padded = -(-tokens // 128) * 128
     dma = pltpu.SemaphoreType.DMA
-    return pl.pallas_call(
+    both = pl.pallas_call(
         functools.partial(kernel, total),
-        out_shape=(jax.ShapeDtypeStruct((32, 512), F32), jax.ShapeDtypeStruct((32, 512), F32)),
+        out_shape=jax.ShapeDtypeStruct((64, 512), F32),
         in_specs=[pl.BlockSpec(memory_space=pl.ANY)] * 3,
-        out_specs=(pl.BlockSpec(memory_space=pltpu.VMEM),) * 2,
+        out_specs=pl.BlockSpec(memory_space=pltpu.VMEM),
         scratch_shapes=[
             pltpu.VMEM((padded, width), BF16),
             pltpu.VMEM((padded, width), BF16),
             pltpu.VMEM((8, 128), I32),
             pltpu.VMEM((2 * width, padded), BF16),
             pltpu.VMEM((512, padded), BF16),
+            pltpu.VMEM((2, 4, 256, 128), F32),
             pltpu.VMEM((4, 2, 256, 128), F32),
             pltpu.VMEM((4, 2, 64, 128), F32),
             pltpu.VMEM((4, 2, 3, 272, 128), I16),
@@ -306,6 +327,7 @@
             dma((4,)),
             dma((8, 8)),
             dma((8,)),
+            dma((8, PARTS)),
             dma((8,)),
             dma((8,)),
             dma((4, 2, 3)),
@@ -323,6 +345,7 @@
             flops=2 * 2 * width * 512 * tokens, bytes_accessed=4 * tokens * width, transcendentals=0
         ),
     )(codes, scale_exp.reshape(width // 128, 128), delta)
+    return both[:32] * (1.0 / total), both[32:] * (1.0 / total**0.5)
 
 
 def solution(mesh):

time: 68.4 us -> 64.2 us (0.939)
  the two profiles are of different devices: /device:TPU:1 before, /device:TPU:96 now
where the time goes in v2:
time: 64.2 us; the launch traced here: 64.1 us
  Pallas kernels  61.9 us (96%)
  other arithmetic  1.53 us (2%)
    pallas_call x1, Pallas kernels, shards(): pl.pallas_call(functools.partial(kernel, total), out_shape=jax.ShapeDtype...  61.9 us
    mul x1, other arithmetic, shards(): return (both[:32] * (1.0 / total), both[32:] * (1.0 / total ** 0.5))  1.53 us

profile of v2, /device:TPU:96, one launch (start us, length us, event | category | flops | bytes accessed | tf_op | source)
XLA Modules:
  0.0 64.1 jit_solution(5687191773571682488)
XLA Ops:
  0.6 61.9 %shard_map.50 = f32[64,512]{1,0:T(8,128)} custom-call(bf16[1200,1024]{1,0:T(8,128)(2,1)} %codes.1, s32[8,128]{1,0:T(8,128)} %bitcast.1, bf16[1200,1024]{1,0:T(8,128)(2,1)} %delta.1), custom_call_target="tpu_custom_call" | custom-call | flops 2516582400 | bytes 4915200 | tf_op jit(solution)/shard_map/pallas_call | solution.py:307
  62.5 1.5 %slice_multiply_fusion = (f32[32,512]{1,0:T(8,128)}, f32[32,512]{1,0:T(8,128)}) fusion(f32[64,512]{1,0:T(8,128)} %shard_map.50), kind=kLoop, calls=%fused_computation | loop fusion | flops 32768 | bytes 262144 | tf_op jit(solution)/shard_map/mul | solution.py:348

commit v3 on v2

--- a/solution.py
+++ b/solution.py
@@ -84,14 +84,14 @@
         pltpu.make_async_copy(codes.at[:, pl.ds(128, width - 128)], xs.at[pl.ds(0, tokens), pl.ds(128, width - 128)], load_sem.at[2]),
         pltpu.make_async_copy(delta, ds.at[pl.ds(0, tokens)], load_sem.at[3]),
     ]
+    barrier = pltpu.get_barrier_semaphore()
+    greet = [along(d) for d in (4, -4, 3, -3, 2, -2, 1, -1)]
+    greet += [{a: lax.rem(lax.axis_index(a) + k, 4)} for a in ("x", "y") for k in (2, 1, 3)]
+    greet += [{"core": 1 - core}]
+    for who in greet:
+        pl.semaphore_signal(barrier, inc=1, device_id=who, device_id_type=MESH)
     for c in loads:
         c.start()
-    barrier = pltpu.get_barrier_semaphore()
-    greet = [{"core": 1 - core}]
-    greet += [along(d) for d in (1, -1, 2, -2, 3, -3, 4, -4)]
-    greet += [{a: lax.rem(lax.axis_index(a) + k, 4)} for a in ("x", "y") for k in (1, 2, 3)]
-    for who in greet:
-        pl.semaphore_signal(barrier, inc=1, device_id=who, device_id_type=MESH)
 
     xs[pl.ds(tokens, padded - tokens), :] = jnp.zeros((padded - tokens, width), BF16)
     ds[pl.ds(tokens, padded - tokens), :] = jnp.zeros((padded - tokens, width), BF16)
@@ -182,19 +182,20 @@
                 q = jnp.where((zlo == a) & (k == n), CHUNKS[a][n], q)
         return q
 
-    axes = (("x", "y"), ("y", "x"))
+    halves = (1 - zhi, zhi)
+
+    def hop(along_x, j):
+        return {"x": jnp.where(along_x, lax.rem(x + j + 1, 4), x), "y": jnp.where(along_x, y, lax.rem(y + j + 1, 4))}
 
     def send1(k, h, j):
-        to = lax.rem(lax.axis_index(axes[h][0]) + j + 1, 4)
         return pltpu.make_async_remote_copy(
             src_ref=s1.at[k, h, j], dst_ref=r1.at[k, h, j], send_sem=q1s.at[k, h, j], recv_sem=q1r.at[k, h, j],
-            device_id={axes[h][0]: to}, device_id_type=MESH)
+            device_id=hop(h == 0, j), device_id_type=MESH)
 
     def send2(k, h, j):
-        to = lax.rem(lax.axis_index(axes[h][1]) + j + 1, 4)
         return pltpu.make_async_remote_copy(
             src_ref=s2.at[k, h, j], dst_ref=r2.at[k, h, j], send_sem=q2s.at[k, h, j], recv_sem=q2r.at[k, h, j],
-            device_id={axes[h][1]: to}, device_id_type=MESH)
+            device_id=hop(h == 1, j), device_id_type=MESH)
 
     def send3(k):
         return pltpu.make_async_remote_copy(
@@ -205,26 +206,27 @@
         q = chunk_of(k)
         right = win[pl.ds(pl.multiple_of(q * 128, 128), 128), :]
 
-        for h in range(2):
-            me = lax.axis_index(axes[h][0])
-            product[h] = lax.dot_general(
-                left[pl.ds(h * width, width), :], right, (((1,), (1,)), ((), ())), preferred_element_type=F32
+        for n, h in enumerate(halves):
+            me = jnp.where(h == 0, x, y)
+            product[n] = lax.dot_general(
+                left[pl.ds(pl.multiple_of(h * width, width), width), :], right,
+                (((1,), (1,)), ((), ())), preferred_element_type=F32,
             ).reshape(4, width // 4, 128)
 
             @pl.loop(0, 3)
-            def _(j, h=h, me=me):
-                whole, eighths = coded(product[h, lax.rem(me + j + 1, 4)], 8)
+            def _(j, n=n, h=h, me=me):
+                whole, eighths = coded(product[n, lax.rem(me + j + 1, 4)], 8)
                 s1[k, h, j, pl.ds(0, 256), :] = whole
                 s1[k, h, j, pl.ds(256, 16), :] = eighths
                 send1(k, h, j).start()
 
-            own1[k, h] = product[h, me]
+            own1[k, h] = product[n, me]
 
     def second(k):
-        for h in range(2):
+        for h in halves:
             for j in range(3):
                 send1(k, h, j).wait_recv()
-            me = lax.axis_index(axes[h][1])
+            me = jnp.where(h == 0, y, x)
             own1[k, h] = own1[k, h] + decoded(r1, (k, h, 0), 8) + decoded(r1, (k, h, 1), 8) + decoded(r1, (k, h, 2), 8)
             for j in range(3):
                 t = lax.rem(me + j + 1, 4)
@@ -235,14 +237,17 @@
             own2[k, h] = own1[k, h, pl.ds(pl.multiple_of(me * 64, 64), 64), :]
 
     def third(k):
-        for h in range(2):
+        for n, h in enumerate(halves):
             for j in range(3):
                 send2(k, h, j).wait_recv()
-            own2[k, h] = own2[k, h] + decoded(r2, (k, h, 0), 2) + decoded(r2, (k, h, 1), 2) + decoded(r2, (k, h, 2), 2)
-        whole, eighths = coded(own2[k, 1 - zhi], 2)
-        s3[k, pl.ds(0, 64), :] = whole
-        s3[k, pl.ds(64, 16), :] = eighths
-        send3(k).start()
+            value = own2[k, h] + decoded(r2, (k, h, 0), 2) + decoded(r2, (k, h, 1), 2) + decoded(r2, (k, h, 2), 2)
+            if n == 0:
+                whole, eighths = coded(value, 2)
+                s3[k, pl.ds(0, 64), :] = whole
+                s3[k, pl.ds(64, 16), :] = eighths
+                send3(k).start()
+            else:
+                own2[k, h] = value
 
     def last(k):
         send3(k).wait_recv()

time: 64.2 us -> 62.5 us (0.974)
  Pallas kernels: 61.9 us -> 60.2 us
    pallas_call x1, Pallas kernels: 61.9 us -> 60.2 us  [shards(): pl.pallas_call(functools.partial(kernel, total), out_shape=jax.ShapeDtype...]
where the time goes in v3:
time: 62.5 us; the launch traced here: 62.4 us
  Pallas kernels  60.2 us (96%)
  other arithmetic  1.53 us (2%)
  between operations  0.64 us (1%)
    pallas_call x1, Pallas kernels, shards(): pl.pallas_call(functools.partial(kernel, total), out_shape=jax.ShapeDtype...  60.2 us
    mul x1, other arithmetic, shards(): return (both[:32] * (1.0 / total), both[32:] * (1.0 / total ** 0.5))  1.53 us

profile of v3, /device:TPU:96, one launch (start us, length us, event | category | flops | bytes accessed | tf_op | source)
XLA Modules:
  0.0 62.4 jit_solution(10557500431647933901)
XLA Ops:
  0.6 60.2 %shard_map.50 = f32[64,512]{1,0:T(8,128)} custom-call(bf16[1200,1024]{1,0:T(8,128)(2,1)} %codes.1, s32[8,128]{1,0:T(8,128)} %bitcast.1, bf16[1200,1024]{1,0:T(8,128)(2,1)} %delta.1), custom_call_target="tpu_custom_call" | custom-call | flops 2516582400 | bytes 4915200 | tf_op jit(solution)/shard_map/pallas_call | solution.py:312
  60.8 1.5 %slice_multiply_fusion = (f32[32,512]{1,0:T(8,128)}, f32[32,512]{1,0:T(8,128)}) fusion(f32[64,512]{1,0:T(8,128)} %shard_map.50), kind=kLoop, calls=%fused_computation | loop fusion | flops 32768 | bytes 262144 | tf_op jit(solution)/shard_map/mul | solution.py:353
